TPU v7x, 128 devices: a whole 4x4x4 slice. The times are simulated.
128 devices in a mesh: table: 2 (over z_lo), batch: 64 (over y, z_hi, x, core).
Axes of the slice: x: 4, y: 4, z: 4 (z_hi: 2, z_lo: 2; z = z_hi * 2 + z_lo), core: 2. Of those that a mesh axis runs over, the one named last changes fastest.
Arguments:
- x_first: bfloat16 [8192, 4096], P('batch', 'table'), may hold values from -6 to 6
- x_layer: bfloat16 [8192, 4096], P('batch', 'table'), may hold values from -6 to 6
- pre_act: bfloat16 [8192, 4096], P('batch', 'table'), may hold values from -8 to 8
- gamma: float32 [4096], P('table'), may hold values from 0.3 to 3
- weight: float32 [4096, 4096], P('table', 'batch'), may hold values from -0.09375 to 0.09375
- cotangent: bfloat16 [8192, 4096], P('batch', 'table'), may hold values from -12 to 12
Outputs:
- grad_first: bfloat16 [8192, 4096], P('batch', 'table')
- grad_layer: bfloat16 [8192, 4096], P('batch', 'table')
- grad_weight: float32 [4096, 4096], P('table', 'batch')
- grad_bias: float32 [4096], P('table')
- grad_gamma: float32 [4096], P('table')
All inputs are finite; a program needn't handle non-finite values.
Results may differ from a plain program's by a relative error of at most 0.005.
Values may be sent and summed in bfloat16 or wider, within the bound.
No kernel may reach another device: no remote copies, remote signals or barrier semaphores. Data moves between devices by JAX's collectives and lax.ppermute only.
A program may use at most 128 MiB of HBM per device.

v0:
```python
import jax
import jax.numpy as jnp
from jax import lax
from jax.experimental import pallas as pl
from jax.experimental.pallas import tpu as pltpu
from jax.sharding import Mesh, PartitionSpec as P

BF = jnp.bfloat16
F32 = jnp.float32
PARAMS = pltpu.CompilerParams(vmem_limit_bytes=20 * 1024 * 1024)
LARGE = pltpu.CompilerParams(vmem_limit_bytes=60 * 1024 * 1024)
ANY = pl.BlockSpec(memory_space=pl.ANY)
VMEM = pl.BlockSpec(memory_space=pltpu.VMEM)
HBM = pl.BlockSpec(memory_space=pltpu.HBM)
EXTRA = 128
BRIEF = pl.CostEstimate(flops=1000, bytes_accessed=1000, transcendentals=0)


def gate_body(first_ref, pre_ref, gamma_ref, cot_ref, gpre_ref, *scratch):
    bufs, sems = scratch[:3], scratch[3]
    rows, width = first_ref.shape
    lanes = gpre_ref.shape[1] - width
    tile = 512
    copies = []
    for j in range(width // tile):
        span = slice(j * tile, (j + 1) * tile)
        for n, ref in enumerate((first_ref, pre_ref, cot_ref)):
            copies.append(pltpu.make_async_copy(ref.at[:, span], bufs[n].at[:, span], sems.at[3 * j + n]))
            copies[-1].start()
    gpre_ref[96:, width:] = jnp.zeros((rows - 96, lanes), BF)
    for j in range(width // tile):
        span = slice(j * tile, (j + 1) * tile)
        for copy in copies[3 * j : 3 * j + 3]:
            copy.wait()
        gamma = gamma_ref[:, span]
        pre = bufs[1][:, span].astype(F32)
        gate = jnp.tanh(gamma * pre)
        hidden = bufs[2][:, span].astype(F32) * bufs[0][:, span].astype(F32)
        turn = pre * (1.0 - gate * gate)
        gpre = (hidden * (gate + gamma * turn)).astype(BF)
        gpre_ref[:, span] = gpre
        sums = jnp.sum(gpre.astype(F32), axis=0, keepdims=True), jnp.sum(hidden * pre * turn, axis=0, keepdims=True)
        for n, rest in enumerate(sums):
            for p in range(3):
                piece = rest.astype(BF)
                rest = rest - piece.astype(F32)
                for i in range(tile // lanes):
                    row = 48 * n + 16 * p + j * (tile // lanes) + i
                    gpre_ref[row : row + 1, width:] = piece[:, i * lanes : (i + 1) * lanes]


def gate_step(x_first, pre_act, gamma, cotangent):
    rows, width = x_first.shape
    buf = pltpu.VMEM((rows, width), BF)
    return pl.pallas_call(
        gate_body,
        in_specs=[ANY, ANY, VMEM, ANY],
        out_specs=VMEM,
        out_shape=jax.ShapeDtypeStruct((rows, width + EXTRA), BF),
        scratch_shapes=[buf, buf, buf, pltpu.SemaphoreType.DMA((3 * width // 512,))],
        compiler_params=LARGE,
        cost_estimate=pl.CostEstimate(flops=rows * width * 20, bytes_accessed=rows * width * 8, transcendentals=rows * width),
        name="gate",
    )(x_first, pre_act, gamma, cotangent)


def first_body(pre_ref, gamma_ref, cot_ref, out_ref):
    pre = pre_ref[...].astype(F32)
    out_ref[...] = (cot_ref[...].astype(F32) * (pre * jnp.tanh(gamma_ref[...] * pre))).astype(BF)


def first_step(pre_act, gamma, cotangent):
    rows, width = pre_act.shape
    tile = 512
    block = pl.BlockSpec((rows, tile), lambda j: (0, j))
    return pl.pallas_call(
        first_body,
        grid=(width // tile,),
        in_specs=[block, pl.BlockSpec((1, tile), lambda j: (0, j)), block],
        out_specs=block,
        out_shape=jax.ShapeDtypeStruct((rows, width), BF),
        compiler_params=LARGE,
        cost_estimate=BRIEF,
        name="first",
    )(pre_act, gamma, cotangent)


LAY = ((0, 0, 2), (1, 0, 2), (3, 0, 2), (2, 0, 1), (2, 1, 1))


def sample_rows(pieces, back, s, span):
    return [pieces[2 * n + s][:, span] for n, place in enumerate(LAY) if place[0] == back]


def load_weights(weights, grid_ref, sems):
    short = grid_ref.shape[0] // 8
    y, h = lax.axis_index("y"), lax.axis_index("h")
    moves = []
    for n, (back, start, size) in enumerate(LAY):
        place_y = lax.rem(y + 4 - back, 4)
        for s in range(size):
            block = place_y * 2 + ((start + s) ^ h)
            place = pl.ds(pl.multiple_of(block * short, short), short)
            source = weights[n].at[s * short : (s + 1) * short]
            moves.append(pltpu.make_async_copy(source, grid_ref.at[place], sems.at[2 * n + s]))
            moves[-1].start()
    return moves


def weight_body(*refs):
    pieces, cols_ref = refs[:10], refs[10]
    results, (out_ref, sems) = refs[11:15], refs[15:]
    pairs, owners, deep, rows = cols_ref.shape
    width = out_ref.shape[1] - EXTRA
    x, c, y = lax.axis_index("x"), lax.axis_index("c"), lax.axis_index("y")
    sends = []

    def hand_out(span):
        for k, result_ref in enumerate(results):
            block = pl.ds(pl.multiple_of(lax.rem(y + k, 4) * 2 * 64, 128), 128)
            sends.append(pltpu.make_async_copy(out_ref.at[block, span], result_ref.at[:, span], sems.at[len(sends)]))
            sends[-1].start()

    order = [(back, s) for back in range(4) for s in range(2)]
    total = 0.0
    for back, s in order:
        total = total + jnp.concatenate(sample_rows(pieces, back, s, slice(width, width + EXTRA))).astype(F32)
    for n in range(2):
        value = total[48 * n : 48 * n + 16] + total[48 * n + 16 : 48 * n + 32] + total[48 * n + 32 : 48 * n + 48]
        high = value.astype(BF)
        low = (value - high.astype(F32)).astype(BF)
        for b in range(pairs * deep // 64):
            out_ref[64 * b + 32 * n : 64 * b + 32 * n + 16, width:] = high
            out_ref[64 * b + 32 * n + 16 : 64 * b + 32 * n + 32, width:] = low
    hand_out(slice(width, width + EXTRA))
    tile = 512
    owner = [lax.rem(x + 4 - back, 4) * 2 + (s ^ c) for back, s in order]
    for j in range(width // tile):
        span = slice(j * tile, (j + 1) * tile)
        samples = jnp.concatenate(sum((sample_rows(pieces, back, s, span) for back, s in order), []))
        for p in range(pairs):
            grid = jnp.concatenate([cols_ref[p, a] for a in owner], axis=1)
            out_ref[p * deep : (p + 1) * deep, span] = jnp.dot(grid, samples, preferred_element_type=F32).astype(BF)
        hand_out(span)
    for send in sends:
        send.wait()


def weight_product(pieces, cols):
    wide = pieces[0].shape[1]
    pairs, _, deep, _ = cols.shape
    return pl.pallas_call(
        weight_body,
        in_specs=[VMEM] * 11,
        out_specs=[HBM] * 4,
        out_shape=[jax.ShapeDtypeStruct((pairs * deep // 4, wide), BF)] * 4,
        scratch_shapes=[
            pltpu.VMEM((pairs * deep, wide), BF),
            pltpu.SemaphoreType.DMA((4 + 4 * ((wide - EXTRA) // 512),)),
        ],
        compiler_params=pltpu.CompilerParams(vmem_limit_bytes=24 * 1024 * 1024),
        cost_estimate=BRIEF,
        name="weight_product",
    )(*pieces, cols)


def layer_body(*refs):
    pieces, weights, (out_ref, samples_ref, grid_ref, sems, more) = refs[:10], refs[10:15], refs[15:]
    width = grid_ref.shape[1]
    pairs, _, deep, rows = out_ref.shape
    x, c = lax.axis_index("x"), lax.axis_index("c")
    moves, copies = load_weights(weights, grid_ref, more), []
    for n, (back, start, size) in enumerate(LAY):
        for s in range(2):
            first = (2 * back + s) * rows + start * rows // 2
            source = pieces[2 * n + s].at[:, :width]
            copies.append(
                pltpu.make_async_copy(source, samples_ref.at[first : first + size * rows // 2], sems.at[2 * n + s])
            )
            copies[-1].start()
    for move in moves:
        move.wait()
    for n, (back, start, size) in enumerate(LAY):
        for s in range(2):
            copies[2 * n + s].wait()
        if size == 1 and start == 0:
            continue
        part = lax.dot_general(
            grid_ref[...],
            samples_ref[2 * back * rows : 2 * (back + 1) * rows],
            (((1,), (1,)), ((), ())),
            preferred_element_type=F32,
        )
        for s in range(2):
            owner = lax.rem(x + 4 - back, 4) * 2 + (s ^ c)
            for p in range(pairs):
                block = part[p * deep : (p + 1) * deep, s * rows : (s + 1) * rows]
                out_ref[p, owner] = block.astype(BF)


def layer_product(pieces, weights):
    rows = pieces[0].shape[0]
    width = weights[0].shape[1]
    deep = 4 * weights[0].shape[0]
    return pl.pallas_call(
        layer_body,
        in_specs=[HBM] * 15,
        out_specs=VMEM,
        out_shape=jax.ShapeDtypeStruct((2, 8, deep // 2, rows), BF),
        scratch_shapes=[
            pltpu.VMEM((8 * rows, width), BF),
            pltpu.VMEM((deep, width), BF),
            pltpu.SemaphoreType.DMA((10,)),
            pltpu.SemaphoreType.DMA((10,)),
        ],
        compiler_params=LARGE,
        cost_estimate=BRIEF,
        name="layer_product",
    )(*pieces, *weights)


def fold_body(one, two, three, four, keep_ref, send_ref, total_ref):
    short = keep_ref.shape[0]
    width = keep_ref.shape[1] - EXTRA
    h = lax.axis_index("h")
    total = one[...].astype(F32)
    for ref in (two, three, four):
        total = total + ref[...].astype(F32)
    total_ref[...] = total
    keep_ref[...] = total_ref[pl.ds(pl.multiple_of(h * short, short), short)]
    send_ref[:, :width] = total_ref[pl.ds(pl.multiple_of((1 - h) * short, short), short), :width].astype(BF)
    for n in range(2):
        value = total[32 * n : 32 * n + 16, width:] + total[32 * n + 16 : 32 * n + 32, width:]
        high = value.astype(BF)
        send_ref[32 * n : 32 * n + 16, width:] = high
        send_ref[32 * n + 16 : 32 * n + 32, width:] = (value - high.astype(F32)).astype(BF)


def fold_parts(parts):
    rows, width = parts[0].shape
    return pl.pallas_call(
        fold_body,
        in_specs=[VMEM] * 4,
        out_specs=[VMEM, VMEM],
        out_shape=[
            jax.ShapeDtypeStruct((rows // 2, width), F32),
            jax.ShapeDtypeStruct((rows // 2, width), BF),
        ],
        scratch_shapes=[pltpu.VMEM((rows, width), F32)],
        compiler_params=PARAMS,
        cost_estimate=BRIEF,
        name="fold",
    )(*parts)


def total_body(keep_ref, came_ref, out_ref, sums_ref):
    width = out_ref.shape[1]
    out_ref[...] = keep_ref[:, :width] + came_ref[:, :width].astype(F32)
    for n in range(2):
        both = keep_ref[32 * n : 32 * n + 32, width:] + came_ref[32 * n : 32 * n + 32, width:].astype(F32)
        sums_ref[n] = both[:16] + both[16:]


def total_parts(keep, came):
    rows, width = keep.shape
    return pl.pallas_call(
        total_body,
        in_specs=[VMEM, VMEM],
        out_specs=[VMEM, VMEM],
        out_shape=[
            jax.ShapeDtypeStruct((rows, width - EXTRA), F32),
            jax.ShapeDtypeStruct((2, 16, EXTRA), F32),
        ],
        compiler_params=PARAMS,
        cost_estimate=BRIEF,
        name="total",
    )(keep, came)


def finish_body(parts_ref, cot_ref, out_ref):
    owners, cols = parts_ref.shape[1], parts_ref.shape[3]
    total = parts_ref[0, :, 0].astype(F32) + parts_ref[1, :, 0].astype(F32)
    total = total.reshape(owners * cols, total.shape[2])
    out_ref[...] = (cot_ref[...].astype(F32) + total.T).astype(BF)


def finish(parts, cotangent):
    pairs, owners, blocks, cols, rows = parts.shape
    wide = owners * cols
    return pl.pallas_call(
        finish_body,
        grid=(blocks,),
        in_specs=[
            pl.BlockSpec((pairs, owners, 1, cols, rows), lambda j: (0, 0, j, 0, 0)),
            pl.BlockSpec((rows, wide), lambda j: (0, j)),
        ],
        out_specs=pl.BlockSpec((rows, wide), lambda j: (0, j)),
        out_shape=jax.ShapeDtypeStruct((rows, blocks * wide), BF),
        compiler_params=PARAMS,
        cost_estimate=BRIEF,
        name="finish",
    )(parts, cotangent)


def ahead(value, axis, size, steps):
    return lax.ppermute(value, axis, [(i, (i + steps) % size) for i in range(size)])


def swap(value, axis, size, bit):
    return lax.ppermute(value, axis, [(i, i ^ bit) for i in range(size)])


def ring_gather(value, axis):
    rows = value.shape[0]
    left, right = ahead(value, axis, 4, 1), ahead(value, axis, 4, 3)
    far_low = ahead(left[: rows // 2], axis, 4, 1)
    far_high = ahead(right[rows // 2 :], axis, 4, 3)
    return [value, left, right, far_low, far_high]


def shards(x_first, x_layer, pre_act, gamma, weight, cotangent):
    both = ("t", "x", "c")
    n_near, pairs = 8, 2
    samples, half = x_first.shape
    cols = weight.shape[1]
    blocks = half // (n_near * cols)
    gamma = gamma[None, :]

    by_owner = x_layer.T.reshape(blocks, n_near, cols, samples).transpose(1, 0, 2, 3)
    by_owner = by_owner.reshape(n_near, blocks * cols, samples)
    sent = jnp.concatenate([by_owner] * pairs, axis=0)
    weight_bf = weight.T.astype(BF)
    x_first, sent, weight_bf = lax.optimization_barrier((x_first, sent, weight_bf))
    came = lax.all_to_all(sent, both, 0, 0, tiled=True).reshape(pairs, n_near, blocks * cols, samples)

    gpre = gate_step(x_first, pre_act, gamma, cotangent)
    own = ring_gather(gpre, "x")
    weight_two = jnp.concatenate([weight_bf, swap(weight_bf, "h", 2, 1)], axis=0)
    weights = ring_gather(weight_two, "y")
    grad_first = first_step(pre_act, gamma, cotangent)

    own, weights, came, grad_first = lax.optimization_barrier((own, weights, came, grad_first))
    pieces = []
    for piece in own:
        pieces += [piece, swap(piece, "c", 2, 1)]

    parts = weight_product(pieces, came)
    pieces, parts = lax.optimization_barrier((pieces, parts))
    weight_parts = [parts[0]] + [ahead(parts[k], "y", 4, k) for k in (1, 2, 3)]
    sent = layer_product(pieces, weights).reshape(pairs * n_near, blocks * cols, samples)
    layer_parts = lax.all_to_all(sent, both, 0, 0, tiled=True)
    kept, folded = fold_parts(weight_parts)
    grad_layer = finish(layer_parts.reshape(pairs, n_near, blocks, cols, samples), cotangent)
    grad_weight, sums = total_parts(kept, swap(folded, "h", 2, 1))
    return grad_first, grad_layer, grad_weight.T, sums[0].reshape(half), sums[1].reshape(half)


def solution(mesh):
    fine = Mesh(mesh.devices.reshape(2, 4, 2, 4, 2), ("t", "y", "h", "x", "c"))
    batch = ("y", "h", "x", "c")
    wide = P(batch, "t")
    return jax.shard_map(
        shards,
        mesh=fine,
        in_specs=(wide, wide, wide, P("t"), P("t", batch), wide),
        out_specs=(wide, wide, P("t", batch), P("t"), P("t")),
        check_vma=False,
    )
```

profile of v0, /device:TPU:0, one launch (start us, length us, event | category | flops | bytes accessed | tf_op | source)
XLA Modules:
  0.0 100.0 jit_solution(3303562559998459962)
XLA Ops:
  0.6 1.1 %convert_bitcast_fusion = bf16[64,2048]{1,0:T(8,128)(2,1)S(1)} fusion(f32[2048,64]{0,1:T(8,128)} %param.10), kind=kLoop, calls=%fused_computation.1 | loop fusion | flops 131072 | bytes 786432 | tf_op jit(solution)/shard_map/convert_element_type | solution.py:332
  1.8 0.1 copy-done.16
  1.8 0.3 copy.13
  2.2 1.1 %pad_maximum_fusion = bf16[16,256,128]{2,1,0:T(8,128)(2,1)} fusion(bf16[8,256,128]{2,1,0:T(8,128)(2,1)S(1)} %bitcast.20), kind=kLoop, calls=%fused_computation | loop fusion | flops 524288 | bytes 1572864 | tf_op jit(solution)/shard_map/concatenate | solution.py:331
  3.2 4.0 %collective-permute-start.4 = (bf16[64,2048]{1,0:T(8,128)(2,1)S(1)}, bf16[64,2048]{1,0:T(8,128)(2,1)S(1)}, u32[]{:S(2)}, u32[]{:S(2)}) collective-permute-start(bf16[64,2048]{1,0:T(8,128)(2,1)S(1)} %convert_bitcast_fusion), channel_id=1, source_target_pairs={{0,8},{8,0},{1,9},{9,1},{2,10},{10,2},{3,11},{11,3},{4,12},{12,4},... | collective-permute-start | bytes 786440 | tf_op jit(solution)/shard_map/ppermute | solution.py:310
  7.2 3.7 %gate.1.refs_0_ = bf16[128,2176]{1,0:T(8,128)(2,1)} custom-call(bf16[128,2048]{1,0:T(8,128)(2,1)} %first_ref, bf16[128,2048]{1,0:T(8,128)(2,1)} %pre_ref.3, f32[1,2048]{1,0:T(1,128)} %bitcast.22, bf16[128,2048]{1,0:T(8,128)(2,1)} %cot_ref.5), custom_call_target="tpu_custom_call" | custom-call | flops 5242880 | bytes 2097152 | tf_op jit(solution)/shard_map/gate/pallas_call | solution.py:55
  10.9 2.8 %collective-permute-start.1 = (bf16[128,2176]{1,0:T(8,128)(2,1)}, bf16[128,2176]{1,0:T(8,128)(2,1)S(1)}, u32[]{:S(2)}, u32[]{:S(2)}) collective-permute-start(bf16[128,2176]{1,0:T(8,128)(2,1)} %gate.1.refs_0_), channel_id=1, source_target_pairs={{0,6},{2,0},{4,2},{6,4},{1,7},{3,1},{5,3},{7,5},{8,14},{10,8},{12,... | collective-permute-start | bytes 1671176 | tf_op jit(solution)/shard_map/ppermute | solution.py:306
  13.7 0.0 collective-permute-start
  13.7 5.1 %all-to-all-start = ((bf16[16,256,128]{2,1,0:T(8,128)(2,1)}), bf16[16,256,128]{2,1,0:T(8,128)(2,1)S(1)}, u32[]{:S(2)}, u32[]{:S(2)}) async-start(bf16[16,256,128]{2,1,0:T(8,128)(2,1)} %pad_maximum_fusion), calls=%async_computation | async-start | bytes 2097152 | tf_op jit(solution)/shard_map/all_to_all | solution.py:334
  18.8 0.0 copy-start.15
  18.8 3.1 %collective-permute-start.6 = (bf16[128,2048]{1,0:T(8,128)(2,1)S(1)}, bf16[128,2048]{1,0:T(8,128)(2,1)S(1)}, u32[]{:S(2)}, u32[]{:S(2)}) collective-permute-start(bf16[128,2048]{1,0:T(8,128)(2,1)S(1)} %constant_dynamic-update-slice_fusion.refs_10_), channel_id=1, source_target_pairs={{0,48},{16,0},{32,16},{48,32},{1,49},{17,1},{33,17},{49,33},{2,50}... | collective-permute-start | bytes 1572872 | tf_op jit(solution)/shard_map/ppermute | solution.py:306
  21.9 0.0 collective-permute-start.5
  21.9 8.5 %collective-permute-done.1.refs_4_ = bf16[128,2176]{1,0:T(8,128)(2,1)S(1)} collective-permute-done((bf16[128,2176]{1,0:T(8,128)(2,1)}, bf16[128,2176]{1,0:T(8,128)(2,1)S(1)}, u32[]{:S(2)}, u32[]{:S(2)}) %collective-permute-start.1) | collective-permute-done | bytes 557088 | tf_op jit(solution)/shard_map/ppermute | solution.py:306
  30.5 3.8 %collective-permute-start.3 = (bf16[64,2176]{1,0:T(8,128)(2,1)S(1)}, bf16[64,2176]{1,0:T(8,128)(2,1)S(1)}, u32[]{:S(2)}, u32[]{:S(2)}) collective-permute-start(bf16[64,2176]{1,0:T(8,128)(2,1)S(1)} %slice.25), channel_id=1, source_target_pairs={{0,6},{2,0},{4,2},{6,4},{1,7},{3,1},{5,3},{7,5},{8,14},{10,8},{12,... | collective-permute-start | bytes 835592 | tf_op jit(solution)/shard_map/ppermute | solution.py:306
  34.3 0.0 collective-permute-done.refs_2_
  34.3 0.1 collective-permute-start.2
  34.4 0.0 collective-permute-done.6.refs_12_
  34.4 3.1 %collective-permute-start.8 = (bf16[64,2048]{1,0:T(8,128)(2,1)S(1)}, bf16[64,2048]{1,0:T(8,128)(2,1)}, u32[]{:S(2)}, u32[]{:S(2)}) collective-permute-start(bf16[64,2048]{1,0:T(8,128)(2,1)S(1)} %slice.27), channel_id=1, source_target_pairs={{0,48},{16,0},{32,16},{48,32},{1,49},{17,1},{33,17},{49,33},{2,50}... | collective-permute-start | bytes 786440 | tf_op jit(solution)/shard_map/ppermute | solution.py:306
  37.5 0.8 copy-done.14
  38.3 0.8 slice.26
  39.1 0.0 collective-permute-start.7
  39.1 3.5 %first.1 = bf16[128,2048]{1,0:T(8,128)(2,1)} custom-call(bf16[128,2048]{1,0:T(8,128)(2,1)} %pre_ref.3, f32[1,2048]{1,0:T(1,128)} %bitcast.23, bf16[128,2048]{1,0:T(8,128)(2,1)} %cot_ref.5), custom_call_target="tpu_custom_call" | custom-call | flops 1000 | bytes 1000 | tf_op jit(solution)/shard_map/first/pallas_call | solution.py:76
  42.6 0.1 collective-permute-done.3.refs_8_
  42.7 3.4 %collective-permute-done.2.refs_6_ = bf16[64,2176]{1,0:T(8,128)(2,1)S(1)} collective-permute-done((bf16[64,2176]{1,0:T(8,128)(2,1)S(1)}, bf16[64,2176]{1,0:T(8,128)(2,1)S(1)}, u32[]{:S(2)}, u32[]{:S(2)}) %collective-permute-start.2) | collective-permute-done | bytes 278560 | tf_op jit(solution)/shard_map/ppermute | solution.py:306
  46.1 2.0 %collective-permute-done.7.refs_13_ = bf16[64,2048]{1,0:T(8,128)(2,1)} collective-permute-done((bf16[64,2048]{1,0:T(8,128)(2,1)}, bf16[64,2048]{1,0:T(8,128)(2,1)}, u32[]{:S(2)}, u32[]{:S(2)}) %collective-permute-start.7) | collective-permute-done | bytes 262176 | tf_op jit(solution)/shard_map/ppermute | solution.py:306
  48.1 0.0 collective-permute-start.9
  48.2 0.5 collective-permute-start.10
  48.7 0.0 collective-permute-start.11
  48.7 0.5 collective-permute-start.12
  49.2 0.0 collective-permute-start.13
  49.2 2.9 %collective-permute-done.12.refs_7_ = bf16[64,2176]{1,0:T(8,128)(2,1)S(1)} collective-permute-done((bf16[64,2176]{1,0:T(8,128)(2,1)S(1)}, bf16[64,2176]{1,0:T(8,128)(2,1)S(1)}, u32[]{:S(2)}, u32[]{:S(2)}) %collective-permute-start.12) | collective-permute-done | bytes 278560 | tf_op jit(solution)/shard_map/ppermute | solution.py:310
  52.1 0.4 collective-permute-done.13.refs_9_
  52.5 0.0 collective-permute-done.9.refs_1_
  52.6 3.9 %weight_product.1 = (bf16[128,2176]{1,0:T(8,128)(2,1)S(1)}, bf16[128,2176]{1,0:T(8,128)(2,1)}, bf16[128,2176]{1,0:T(8,128)(2,1)}, bf16[128,2176]{1,0:T(8,128)(2,1)}) custom-call(bf16[128,2176]{1,0:T(8,128)(2,1)S(1)} %copy-done, bf16[128,2176]{1,0:T(8,128)(2,1)S(1)} %collective-permute-done.9.refs_1_, bf16[128,2176]{1,0:T(8,128)(2,1)S(1)} %collective-permute-done.refs_2_, ...), custom_call_target="tpu_custom_call" | custom-call | flops 1000 | bytes 1000 | tf_op jit(solution)/shard_map/weight_product/pallas_call | solution.py:152
  56.6 0.8 copy-done.11
  57.4 2.6 %collective-permute-start.15 = (bf16[128,2176]{1,0:T(8,128)(2,1)}, bf16[128,2176]{1,0:T(8,128)(2,1)S(1)}, u32[]{:S(2)}, u32[]{:S(2)}) collective-permute-start(bf16[128,2176]{1,0:T(8,128)(2,1)} %get-tuple-element.73), channel_id=1, source_target_pairs={{0,32},{16,48},{32,0},{48,16},{1,33},{17,49},{33,1},{49,17},{2,34}... | collective-permute-start | bytes 1671176 | tf_op jit(solution)/shard_map/ppermute | solution.py:306
  60.0 1.3 %collective-permute-start.16 = (bf16[128,2176]{1,0:T(8,128)(2,1)}, bf16[128,2176]{1,0:T(8,128)(2,1)S(1)}, u32[]{:S(2)}, u32[]{:S(2)}) collective-permute-start(bf16[128,2176]{1,0:T(8,128)(2,1)} %get-tuple-element.74), channel_id=1, source_target_pairs={{0,48},{16,0},{32,16},{48,32},{1,49},{17,1},{33,17},{49,33},{2,50}... | collective-permute-start | bytes 1671176 | tf_op jit(solution)/shard_map/ppermute | solution.py:306
  61.3 8.9 %layer_product.1 = bf16[2,8,256,128]{3,2,1,0:T(8,128)(2,1)} custom-call(bf16[128,2176]{1,0:T(8,128)(2,1)} %gate.1.refs_0_, bf16[128,2176]{1,0:T(8,128)(2,1)} %copy-done.4, bf16[128,2176]{1,0:T(8,128)(2,1)} %copy-done.3, bf16[128,2176]{1,0:T(8,128)(2,1)} %copy-done.5, bf16[128,2176]{1,0:T(8,128)(2,1)} %copy-done.2, bf16[128,2176]{1,0:T(8,128)(2,1)} %copy-done.6, ...), custom_call_target="tpu_custom_call" | custom-call | flops 1000 | bytes 1000 | tf_op jit(solution)/shard_map/layer_product/pallas_call | solution.py:205
  70.3 4.6 %all-to-all-start.1 = ((bf16[16,256,128]{2,1,0:T(8,128)(2,1)}), bf16[16,256,128]{2,1,0:T(8,128)(2,1)S(1)}, u32[]{:S(2)}, u32[]{:S(2)}) async-start(bf16[16,256,128]{2,1,0:T(8,128)(2,1)} %bitcast.19), calls=%async_computation.1 | async-start | bytes 2097152 | tf_op jit(solution)/shard_map/all_to_all | solution.py:351
  74.9 10.6 %collective-permute-done.14.two = bf16[128,2176]{1,0:T(8,128)(2,1)S(1)} collective-permute-done((bf16[128,2176]{1,0:T(8,128)(2,1)}, bf16[128,2176]{1,0:T(8,128)(2,1)S(1)}, u32[]{:S(2)}, u32[]{:S(2)}) %collective-permute-start.14) | collective-permute-done | bytes 557088 | tf_op jit(solution)/shard_map/ppermute | solution.py:306
  85.4 0.6 collective-permute-done.16.four
  86.0 0.6 fold.1
  86.6 0.0 copy-start.1
  86.6 1.2 %collective-permute-start.17 = (bf16[64,2176]{1,0:T(8,128)(2,1)S(1)}, bf16[64,2176]{1,0:T(8,128)(2,1)S(1)}, u32[]{:S(2)}, u32[]{:S(2)}) collective-permute-start(bf16[64,2176]{1,0:T(8,128)(2,1)S(1)} %get-tuple-element.76), channel_id=1, source_target_pairs={{0,8},{8,0},{1,9},{9,1},{2,10},{10,2},{3,11},{11,3},{4,12},{12,4},... | collective-permute-start | bytes 835592 | tf_op jit(solution)/shard_map/ppermute | solution.py:310
  87.9 8.9 %collective-permute-done.17.came_ref = bf16[64,2176]{1,0:T(8,128)(2,1)S(1)} collective-permute-done((bf16[64,2176]{1,0:T(8,128)(2,1)S(1)}, bf16[64,2176]{1,0:T(8,128)(2,1)S(1)}, u32[]{:S(2)}, u32[]{:S(2)}) %collective-permute-start.17) | collective-permute-done | bytes 278560 | tf_op jit(solution)/shard_map/ppermute | solution.py:310
  96.7 0.8 total.1
  97.6 0.6 slice_bitcast_fusion
  98.2 1.9 %finish.1 = bf16[128,2048]{1,0:T(8,128)(2,1)} custom-call(bf16[2,8,4,64,128]{4,3,2,1,0:T(8,128)(2,1)S(1)} %bitcast.17, bf16[128,2048]{1,0:T(8,128)(2,1)S(1)} %copy-done.1), custom_call_target="tpu_custom_call" | custom-call | flops 1000 | bytes 1000 | tf_op jit(solution)/shard_map/finish/pallas_call | solution.py:290
  (44 shorter events, 0.2 us)
Async XLA Ops:
  0.6 1.2 %copy-start.16 = (bf16[128,2048]{1,0:T(8,128)(2,1)S(1)}, bf16[128,2048]{1,0:T(8,128)(2,1)}, u32[]{:S(2)}) copy-start(bf16[128,2048]{1,0:T(8,128)(2,1)} %param.7) | copy-start | bytes 1572868
  3.2 15.6 %collective-permute-start.4 = (bf16[64,2048]{1,0:T(8,128)(2,1)S(1)}, bf16[64,2048]{1,0:T(8,128)(2,1)S(1)}, u32[]{:S(2)}, u32[]{:S(2)}) collective-permute-start(bf16[64,2048]{1,0:T(8,128)(2,1)S(1)} %convert_bitcast_fusion), channel_id=1, source_target_pairs={{0,8},{8,0},{1,9},{9,1},{2,10},{10,2},{3,11},{11,3},{4,12},{12,4},... | collective-permute-start | bytes 786440 | tf_op jit(solution)/shard_map/ppermute | solution.py:310
  10.9 19.6 %collective-permute-start.1 = (bf16[128,2176]{1,0:T(8,128)(2,1)}, bf16[128,2176]{1,0:T(8,128)(2,1)S(1)}, u32[]{:S(2)}, u32[]{:S(2)}) collective-permute-start(bf16[128,2176]{1,0:T(8,128)(2,1)} %gate.1.refs_0_), channel_id=1, source_target_pairs={{0,6},{2,0},{4,2},{6,4},{1,7},{3,1},{5,3},{7,5},{8,14},{10,8},{12,... | collective-permute-start | bytes 1671176 | tf_op jit(solution)/shard_map/ppermute | solution.py:306
  13.7 20.6 %collective-permute-start = (bf16[128,2176]{1,0:T(8,128)(2,1)}, bf16[128,2176]{1,0:T(8,128)(2,1)S(1)}, u32[]{:S(2)}, u32[]{:S(2)}) collective-permute-start(bf16[128,2176]{1,0:T(8,128)(2,1)} %gate.1.refs_0_), channel_id=1, source_target_pairs={{0,2},{2,4},{4,6},{6,0},{1,3},{3,5},{5,7},{7,1},{8,10},{10,12},{12... | collective-permute-start | bytes 1671176 | tf_op jit(solution)/shard_map/ppermute | solution.py:306
  13.7 32.4 %all-to-all-start = ((bf16[16,256,128]{2,1,0:T(8,128)(2,1)}), bf16[16,256,128]{2,1,0:T(8,128)(2,1)S(1)}, u32[]{:S(2)}, u32[]{:S(2)}) async-start(bf16[16,256,128]{2,1,0:T(8,128)(2,1)} %pad_maximum_fusion), calls=%async_computation | async-start | bytes 2097152 | tf_op jit(solution)/shard_map/all_to_all | solution.py:334
  18.8 20.2 %copy-start.15 = (bf16[128,2048]{1,0:T(8,128)(2,1)}, bf16[128,2048]{1,0:T(8,128)(2,1)S(1)}, u32[]{:S(2)}) copy-start(bf16[128,2048]{1,0:T(8,128)(2,1)S(1)} %constant_dynamic-update-slice_fusion.refs_10_) | copy-start | bytes 1572868
  18.8 15.5 %collective-permute-start.6 = (bf16[128,2048]{1,0:T(8,128)(2,1)S(1)}, bf16[128,2048]{1,0:T(8,128)(2,1)S(1)}, u32[]{:S(2)}, u32[]{:S(2)}) collective-permute-start(bf16[128,2048]{1,0:T(8,128)(2,1)S(1)} %constant_dynamic-update-slice_fusion.refs_10_), channel_id=1, source_target_pairs={{0,48},{16,0},{32,16},{48,32},{1,49},{17,1},{33,17},{49,33},{2,50}... | collective-permute-start | bytes 1572872 | tf_op jit(solution)/shard_map/ppermute | solution.py:306
  21.9 15.6 %collective-permute-start.5 = (bf16[128,2048]{1,0:T(8,128)(2,1)S(1)}, bf16[128,2048]{1,0:T(8,128)(2,1)S(1)}, u32[]{:S(2)}, u32[]{:S(2)}) collective-permute-start(bf16[128,2048]{1,0:T(8,128)(2,1)S(1)} %constant_dynamic-update-slice_fusion.refs_10_), channel_id=1, source_target_pairs={{0,16},{16,32},{32,48},{48,0},{1,17},{17,33},{33,49},{49,1},{2,18}... | collective-permute-start | bytes 1572872 | tf_op jit(solution)/shard_map/ppermute | solution.py:306
  30.4 22.1 %copy-start.2 = (bf16[128,2176]{1,0:T(8,128)(2,1)}, bf16[128,2176]{1,0:T(8,128)(2,1)S(1)}, u32[]{:S(2)}) copy-start(bf16[128,2176]{1,0:T(8,128)(2,1)S(1)} %collective-permute-done.1.refs_4_) | copy-start | bytes 1671172
  30.5 12.2 %collective-permute-start.3 = (bf16[64,2176]{1,0:T(8,128)(2,1)S(1)}, bf16[64,2176]{1,0:T(8,128)(2,1)S(1)}, u32[]{:S(2)}, u32[]{:S(2)}) collective-permute-start(bf16[64,2176]{1,0:T(8,128)(2,1)S(1)} %slice.25), channel_id=1, source_target_pairs={{0,6},{2,0},{4,2},{6,4},{1,7},{3,1},{5,3},{7,5},{8,14},{10,8},{12,... | collective-permute-start | bytes 835592 | tf_op jit(solution)/shard_map/ppermute | solution.py:306
  34.3 18.3 %copy-start.3 = (bf16[128,2176]{1,0:T(8,128)(2,1)}, bf16[128,2176]{1,0:T(8,128)(2,1)S(1)}, u32[]{:S(2)}) copy-start(bf16[128,2176]{1,0:T(8,128)(2,1)S(1)} %collective-permute-done.refs_2_) | copy-start | bytes 1671172
  34.3 11.8 %collective-permute-start.2 = (bf16[64,2176]{1,0:T(8,128)(2,1)S(1)}, bf16[64,2176]{1,0:T(8,128)(2,1)S(1)}, u32[]{:S(2)}, u32[]{:S(2)}) collective-permute-start(bf16[64,2176]{1,0:T(8,128)(2,1)S(1)} %slice.24), channel_id=1, source_target_pairs={{0,2},{2,4},{4,6},{6,0},{1,3},{3,5},{5,7},{7,1},{8,10},{10,12},{12... | collective-permute-start | bytes 835592 | tf_op jit(solution)/shard_map/ppermute | solution.py:306
  34.4 4.7 %copy-start.13 = (bf16[128,2048]{1,0:T(8,128)(2,1)}, bf16[128,2048]{1,0:T(8,128)(2,1)S(1)}, u32[]{:S(2)}) copy-start(bf16[128,2048]{1,0:T(8,128)(2,1)S(1)} %collective-permute-done.6.refs_12_) | copy-start | bytes 1572868
  34.4 11.7 %collective-permute-start.8 = (bf16[64,2048]{1,0:T(8,128)(2,1)S(1)}, bf16[64,2048]{1,0:T(8,128)(2,1)}, u32[]{:S(2)}, u32[]{:S(2)}) collective-permute-start(bf16[64,2048]{1,0:T(8,128)(2,1)S(1)} %slice.27), channel_id=1, source_target_pairs={{0,48},{16,0},{32,16},{48,32},{1,49},{17,1},{33,17},{49,33},{2,50}... | collective-permute-start | bytes 786440 | tf_op jit(solution)/shard_map/ppermute | solution.py:306
  37.5 0.8 copy-start.14
  39.1 9.1 %copy-start = (bf16[128,2176]{1,0:T(8,128)(2,1)S(1)}, bf16[128,2176]{1,0:T(8,128)(2,1)}, u32[]{:S(2)}) copy-start(bf16[128,2176]{1,0:T(8,128)(2,1)} %gate.1.refs_0_) | copy-start | bytes 1671172
  39.1 9.1 %collective-permute-start.7 = (bf16[64,2048]{1,0:T(8,128)(2,1)}, bf16[64,2048]{1,0:T(8,128)(2,1)}, u32[]{:S(2)}, u32[]{:S(2)}) collective-permute-start(bf16[64,2048]{1,0:T(8,128)(2,1)} %slice.26), channel_id=1, source_target_pairs={{0,16},{16,32},{32,48},{48,0},{1,17},{17,33},{33,49},{49,1},{2,18}... | collective-permute-start | bytes 786440 | tf_op jit(solution)/shard_map/ppermute | solution.py:306
  42.7 13.8 %copy-start.7 = (bf16[64,2176]{1,0:T(8,128)(2,1)}, bf16[64,2176]{1,0:T(8,128)(2,1)S(1)}, u32[]{:S(2)}) copy-start(bf16[64,2176]{1,0:T(8,128)(2,1)S(1)} %collective-permute-done.3.refs_8_) | copy-start | bytes 835588
  46.1 10.4 %copy-start.8 = (bf16[64,2176]{1,0:T(8,128)(2,1)}, bf16[64,2176]{1,0:T(8,128)(2,1)S(1)}, u32[]{:S(2)}) copy-start(bf16[64,2176]{1,0:T(8,128)(2,1)S(1)} %collective-permute-done.2.refs_6_) | copy-start | bytes 835588
  48.1 4.4 %collective-permute-start.9 = (bf16[128,2176]{1,0:T(8,128)(2,1)S(1)}, bf16[128,2176]{1,0:T(8,128)(2,1)S(1)}, u32[]{:S(2)}, u32[]{:S(2)}) collective-permute-start(bf16[128,2176]{1,0:T(8,128)(2,1)S(1)} %copy-done), channel_id=1, source_target_pairs={{0,1},{1,0},{2,3},{3,2},{4,5},{5,4},{6,7},{7,6},{8,9},{9,8},{10,11... | collective-permute-start | bytes 1671176 | tf_op jit(solution)/shard_map/ppermute | solution.py:310
  48.2 4.4 %collective-permute-start.10 = (bf16[128,2176]{1,0:T(8,128)(2,1)S(1)}, bf16[128,2176]{1,0:T(8,128)(2,1)S(1)}, u32[]{:S(2)}, u32[]{:S(2)}) collective-permute-start(bf16[128,2176]{1,0:T(8,128)(2,1)S(1)} %collective-permute-done.refs_2_), channel_id=1, source_target_pairs={{0,1},{1,0},{2,3},{3,2},{4,5},{5,4},{6,7},{7,6},{8,9},{9,8},{10,11... | collective-permute-start | bytes 1671176 | tf_op jit(solution)/shard_map/ppermute | solution.py:310
  48.7 3.9 %collective-permute-start.11 = (bf16[128,2176]{1,0:T(8,128)(2,1)S(1)}, bf16[128,2176]{1,0:T(8,128)(2,1)S(1)}, u32[]{:S(2)}, u32[]{:S(2)}) collective-permute-start(bf16[128,2176]{1,0:T(8,128)(2,1)S(1)} %collective-permute-done.1.refs_4_), channel_id=1, source_target_pairs={{0,1},{1,0},{2,3},{3,2},{4,5},{5,4},{6,7},{7,6},{8,9},{9,8},{10,11... | collective-permute-start | bytes 1671176 | tf_op jit(solution)/shard_map/ppermute | solution.py:310
  48.7 3.4 %collective-permute-start.12 = (bf16[64,2176]{1,0:T(8,128)(2,1)S(1)}, bf16[64,2176]{1,0:T(8,128)(2,1)S(1)}, u32[]{:S(2)}, u32[]{:S(2)}) collective-permute-start(bf16[64,2176]{1,0:T(8,128)(2,1)S(1)} %collective-permute-done.2.refs_6_), channel_id=1, source_target_pairs={{0,1},{1,0},{2,3},{3,2},{4,5},{5,4},{6,7},{7,6},{8,9},{9,8},{10,11... | collective-permute-start | bytes 835592 | tf_op jit(solution)/shard_map/ppermute | solution.py:310
  49.2 3.3 %collective-permute-start.13 = (bf16[64,2176]{1,0:T(8,128)(2,1)S(1)}, bf16[64,2176]{1,0:T(8,128)(2,1)S(1)}, u32[]{:S(2)}, u32[]{:S(2)}) collective-permute-start(bf16[64,2176]{1,0:T(8,128)(2,1)S(1)} %collective-permute-done.3.refs_8_), channel_id=1, source_target_pairs={{0,1},{1,0},{2,3},{3,2},{4,5},{5,4},{6,7},{7,6},{8,9},{9,8},{10,11... | collective-permute-start | bytes 835592 | tf_op jit(solution)/shard_map/ppermute | solution.py:310
  52.1 4.4 %copy-start.9 = (bf16[64,2176]{1,0:T(8,128)(2,1)}, bf16[64,2176]{1,0:T(8,128)(2,1)S(1)}, u32[]{:S(2)}) copy-start(bf16[64,2176]{1,0:T(8,128)(2,1)S(1)} %collective-permute-done.12.refs_7_) | copy-start | bytes 835588
  52.5 4.0 %copy-start.10 = (bf16[64,2176]{1,0:T(8,128)(2,1)}, bf16[64,2176]{1,0:T(8,128)(2,1)S(1)}, u32[]{:S(2)}) copy-start(bf16[64,2176]{1,0:T(8,128)(2,1)S(1)} %collective-permute-done.13.refs_9_) | copy-start | bytes 835588
  52.5 4.0 %copy-start.4 = (bf16[128,2176]{1,0:T(8,128)(2,1)}, bf16[128,2176]{1,0:T(8,128)(2,1)S(1)}, u32[]{:S(2)}) copy-start(bf16[128,2176]{1,0:T(8,128)(2,1)S(1)} %collective-permute-done.9.refs_1_) | copy-start | bytes 1671172
  52.5 4.0 %copy-start.5 = (bf16[128,2176]{1,0:T(8,128)(2,1)}, bf16[128,2176]{1,0:T(8,128)(2,1)S(1)}, u32[]{:S(2)}) copy-start(bf16[128,2176]{1,0:T(8,128)(2,1)S(1)} %collective-permute-done.10.refs_3_) | copy-start | bytes 1671172
  52.6 4.0 %copy-start.6 = (bf16[128,2176]{1,0:T(8,128)(2,1)}, bf16[128,2176]{1,0:T(8,128)(2,1)S(1)}, u32[]{:S(2)}) copy-start(bf16[128,2176]{1,0:T(8,128)(2,1)S(1)} %collective-permute-done.11.refs_5_) | copy-start | bytes 1671172
  56.6 0.8 copy-start.11
  57.4 28.0 %collective-permute-start.14 = (bf16[128,2176]{1,0:T(8,128)(2,1)}, bf16[128,2176]{1,0:T(8,128)(2,1)S(1)}, u32[]{:S(2)}, u32[]{:S(2)}) collective-permute-start(bf16[128,2176]{1,0:T(8,128)(2,1)} %get-tuple-element.72), channel_id=1, source_target_pairs={{0,16},{16,32},{32,48},{48,0},{1,17},{17,33},{33,49},{49,1},{2,18}... | collective-permute-start | bytes 1671176 | tf_op jit(solution)/shard_map/ppermute | solution.py:306
  57.4 28.0 %collective-permute-start.15 = (bf16[128,2176]{1,0:T(8,128)(2,1)}, bf16[128,2176]{1,0:T(8,128)(2,1)S(1)}, u32[]{:S(2)}, u32[]{:S(2)}) collective-permute-start(bf16[128,2176]{1,0:T(8,128)(2,1)} %get-tuple-element.73), channel_id=1, source_target_pairs={{0,32},{16,48},{32,0},{48,16},{1,33},{17,49},{33,1},{49,17},{2,34}... | collective-permute-start | bytes 1671176 | tf_op jit(solution)/shard_map/ppermute | solution.py:306
  60.0 26.1 %collective-permute-start.16 = (bf16[128,2176]{1,0:T(8,128)(2,1)}, bf16[128,2176]{1,0:T(8,128)(2,1)S(1)}, u32[]{:S(2)}, u32[]{:S(2)}) collective-permute-start(bf16[128,2176]{1,0:T(8,128)(2,1)} %get-tuple-element.74), channel_id=1, source_target_pairs={{0,48},{16,0},{32,16},{48,32},{1,49},{17,1},{33,17},{49,33},{2,50}... | collective-permute-start | bytes 1671176 | tf_op jit(solution)/shard_map/ppermute | solution.py:306
  70.3 15.8 %copy-start.12 = (bf16[128,2176]{1,0:T(8,128)(2,1)S(1)}, bf16[128,2176]{1,0:T(8,128)(2,1)}, u32[]{:S(2)}) copy-start(bf16[128,2176]{1,0:T(8,128)(2,1)} %copy-done.11) | copy-start | bytes 1671172
  70.3 27.9 %all-to-all-start.1 = ((bf16[16,256,128]{2,1,0:T(8,128)(2,1)}), bf16[16,256,128]{2,1,0:T(8,128)(2,1)S(1)}, u32[]{:S(2)}, u32[]{:S(2)}) async-start(bf16[16,256,128]{2,1,0:T(8,128)(2,1)} %bitcast.19), calls=%async_computation.1 | async-start | bytes 2097152 | tf_op jit(solution)/shard_map/all_to_all | solution.py:351
  86.6 11.6 %copy-start.1 = (bf16[128,2048]{1,0:T(8,128)(2,1)S(1)}, bf16[128,2048]{1,0:T(8,128)(2,1)}, u32[]{:S(2)}) copy-start(bf16[128,2048]{1,0:T(8,128)(2,1)} %cot_ref.5) | copy-start | bytes 1572868
  86.6 10.1 %collective-permute-start.17 = (bf16[64,2176]{1,0:T(8,128)(2,1)S(1)}, bf16[64,2176]{1,0:T(8,128)(2,1)S(1)}, u32[]{:S(2)}, u32[]{:S(2)}) collective-permute-start(bf16[64,2176]{1,0:T(8,128)(2,1)S(1)} %get-tuple-element.76), channel_id=1, source_target_pairs={{0,8},{8,0},{1,9},{9,1},{2,10},{10,2},{3,11},{11,3},{4,12},{12,4},... | collective-permute-start | bytes 835592 | tf_op jit(solution)/shard_map/ppermute | solution.py:310
where the time goes:
time: 100 us
  waiting for transfers between devices  37.4 us (37%)
  starting transfers between devices  32.7 us (33%)
  Pallas kernels  23.3 us (23%)
  local copies, waits for them, and re-layouts  3.49 us (3%)
  other arithmetic  2.22 us (2%)
    ppermute x11, waiting for transfers between devices, ahead(): lax.ppermute(value, axis, [(i, (i + steps) % size) for i in range(size)])  25.2 us
    ppermute x11, starting transfers between devices, ahead(): lax.ppermute(value, axis, [(i, (i + steps) % size) for i in range(size)])  16.8 us
    ppermute x7, waiting for transfers between devices, swap(): return lax.ppermute(value, axis, [(i, i ^ bit) for i in range(size)])  12.2 us
    pallas_call x1, Pallas kernels, layer_product(): pl.pallas_call(layer_body, in_specs=[HBM] * 15, out_specs=VMEM, out_shape...  8.94 us
    ppermute x7, starting transfers between devices, swap(): return lax.ppermute(value, axis, [(i, i ^ bit) for i in range(size)])  6.23 us
    all_to_all x1, starting transfers between devices, shards(): lax.all_to_all(sent, both, 0, 0, tiled=True)  5.07 us
    all_to_all x1, starting transfers between devices, shards(): layer_parts = lax.all_to_all(sent, both, 0, 0, tiled=True)  4.59 us
    pallas_call x1, Pallas kernels, weight_product(): pl.pallas_call(weight_body, in_specs=[VMEM] * 11, out_specs=[HBM] * 4, ou...  3.94 us
  transfers between devices with their start and end apart: 20, of which 9 were waited for; matrix products, arithmetic and copies ran while one was open for 1% of the time, Pallas kernels for 17%

commit v1 on v0

--- a/solution.py
+++ b/solution.py
@@ -17,7 +17,7 @@
 
 
 def gate_body(first_ref, pre_ref, gamma_ref, cot_ref, gpre_ref, *scratch):
-    bufs, sems = scratch[:3], scratch[3]
+    bufs, rows_ref, sems = scratch[:3], scratch[3], scratch[4]
     rows, width = first_ref.shape
     lanes = gpre_ref.shape[1] - width
     tile = 512
@@ -27,7 +27,7 @@
         for n, ref in enumerate((first_ref, pre_ref, cot_ref)):
             copies.append(pltpu.make_async_copy(ref.at[:, span], bufs[n].at[:, span], sems.at[3 * j + n]))
             copies[-1].start()
-    gpre_ref[96:, width:] = jnp.zeros((rows - 96, lanes), BF)
+    rows_ref[96:] = jnp.zeros((rows - 96, lanes), F32)
     for j in range(width // tile):
         span = slice(j * tile, (j + 1) * tile)
         for copy in copies[3 * j : 3 * j + 3]:
@@ -42,11 +42,12 @@
         sums = jnp.sum(gpre.astype(F32), axis=0, keepdims=True), jnp.sum(hidden * pre * turn, axis=0, keepdims=True)
         for n, rest in enumerate(sums):
             for p in range(3):
-                piece = rest.astype(BF)
-                rest = rest - piece.astype(F32)
+                piece = rest.astype(BF).astype(F32)
+                rest = rest - piece
                 for i in range(tile // lanes):
                     row = 48 * n + 16 * p + j * (tile // lanes) + i
-                    gpre_ref[row : row + 1, width:] = piece[:, i * lanes : (i + 1) * lanes]
+                    rows_ref[row : row + 1] = piece[:, i * lanes : (i + 1) * lanes]
+    gpre_ref[:, width:] = rows_ref[...].astype(BF)
 
 
 def gate_step(x_first, pre_act, gamma, cotangent):
@@ -57,7 +58,7 @@
         in_specs=[ANY, ANY, VMEM, ANY],
         out_specs=VMEM,
         out_shape=jax.ShapeDtypeStruct((rows, width + EXTRA), BF),
-        scratch_shapes=[buf, buf, buf, pltpu.SemaphoreType.DMA((3 * width // 512,))],
+        scratch_shapes=[buf, buf, buf, pltpu.VMEM((rows, EXTRA), F32), pltpu.SemaphoreType.DMA((3 * width // 512,))],
         compiler_params=LARGE,
         cost_estimate=pl.CostEstimate(flops=rows * width * 20, bytes_accessed=rows * width * 8, transcendentals=rows * width),
         name="gate",

time: 100 us -> 100 us (level)
  no operation moved by 1% of the time
where the time goes in v1:
time: 100 us; the launch traced here: 99.8 us
  waiting for transfers between devices  37.5 us (38%)
  starting transfers between devices  32.7 us (33%)
  Pallas kernels  23.1 us (23%)
  local copies, waits for them, and re-layouts  3.49 us (3%)
  other arithmetic  2.22 us (2%)
    ppermute x11, waiting for transfers between devices, ahead(): lax.ppermute(value, axis, [(i, (i + steps) % size) for i in range(size)])  25.2 us
    ppermute x11, starting transfers between devices, ahead(): lax.ppermute(value, axis, [(i, (i + steps) % size) for i in range(size)])  16.8 us
    ppermute x7, waiting for transfers between devices, swap(): return lax.ppermute(value, axis, [(i, i ^ bit) for i in range(size)])  12.2 us
    pallas_call x1, Pallas kernels, layer_product(): pl.pallas_call(layer_body, in_specs=[HBM] * 15, out_specs=VMEM, out_shape...  8.94 us
    ppermute x7, starting transfers between devices, swap(): return lax.ppermute(value, axis, [(i, i ^ bit) for i in range(size)])  6.22 us
    all_to_all x1, starting transfers between devices, shards(): lax.all_to_all(sent, both, 0, 0, tiled=True)  5.07 us
    all_to_all x1, starting transfers between devices, shards(): layer_parts = lax.all_to_all(sent, both, 0, 0, tiled=True)  4.58 us
    pallas_call x1, Pallas kernels, weight_product(): pl.pallas_call(weight_body, in_specs=[VMEM] * 11, out_specs=[HBM] * 4, ou...  3.94 us
  transfers between devices with their start and end apart: 20, of which 9 were waited for; matrix products, arithmetic and copies ran while one was open for 1% of the time, Pallas kernels for 17%

profile of v1, /device:TPU:0, one launch (start us, length us, event | category | flops | bytes accessed | tf_op | source)
XLA Modules:
  0.0 99.8 jit_solution(14487013181013865730)
XLA Ops:
  0.6 1.1 %convert_bitcast_fusion = bf16[64,2048]{1,0:T(8,128)(2,1)S(1)} fusion(f32[2048,64]{0,1:T(8,128)} %param.10), kind=kLoop, calls=%fused_computation.1 | loop fusion | flops 131072 | bytes 786432 | tf_op jit(solution)/shard_map/convert_element_type | solution.py:333
  1.8 0.1 copy-done.16
  1.8 0.3 copy.13
  2.2 1.1 %pad_maximum_fusion = bf16[16,256,128]{2,1,0:T(8,128)(2,1)} fusion(bf16[8,256,128]{2,1,0:T(8,128)(2,1)S(1)} %bitcast.20), kind=kLoop, calls=%fused_computation | loop fusion | flops 524288 | bytes 1572864 | tf_op jit(solution)/shard_map/concatenate | solution.py:332
  3.2 4.0 %collective-permute-start.4 = (bf16[64,2048]{1,0:T(8,128)(2,1)S(1)}, bf16[64,2048]{1,0:T(8,128)(2,1)S(1)}, u32[]{:S(2)}, u32[]{:S(2)}) collective-permute-start(bf16[64,2048]{1,0:T(8,128)(2,1)S(1)} %convert_bitcast_fusion), channel_id=1, source_target_pairs={{0,8},{8,0},{1,9},{9,1},{2,10},{10,2},{3,11},{11,3},{4,12},{12,4},... | collective-permute-start | bytes 786440 | tf_op jit(solution)/shard_map/ppermute | solution.py:311
  7.2 3.4 %gate.1.refs_0_ = bf16[128,2176]{1,0:T(8,128)(2,1)} custom-call(bf16[128,2048]{1,0:T(8,128)(2,1)} %first_ref, bf16[128,2048]{1,0:T(8,128)(2,1)} %pre_ref.3, f32[1,2048]{1,0:T(1,128)} %bitcast.22, bf16[128,2048]{1,0:T(8,128)(2,1)} %cot_ref.5), custom_call_target="tpu_custom_call" | custom-call | flops 5242880 | bytes 2097152 | tf_op jit(solution)/shard_map/gate/pallas_call | solution.py:56
  10.6 2.8 %collective-permute-start.1 = (bf16[128,2176]{1,0:T(8,128)(2,1)}, bf16[128,2176]{1,0:T(8,128)(2,1)S(1)}, u32[]{:S(2)}, u32[]{:S(2)}) collective-permute-start(bf16[128,2176]{1,0:T(8,128)(2,1)} %gate.1.refs_0_), channel_id=1, source_target_pairs={{0,6},{2,0},{4,2},{6,4},{1,7},{3,1},{5,3},{7,5},{8,14},{10,8},{12,... | collective-permute-start | bytes 1671176 | tf_op jit(solution)/shard_map/ppermute | solution.py:307
  13.5 0.0 collective-permute-start
  13.5 5.1 %all-to-all-start = ((bf16[16,256,128]{2,1,0:T(8,128)(2,1)}), bf16[16,256,128]{2,1,0:T(8,128)(2,1)S(1)}, u32[]{:S(2)}, u32[]{:S(2)}) async-start(bf16[16,256,128]{2,1,0:T(8,128)(2,1)} %pad_maximum_fusion), calls=%async_computation | async-start | bytes 2097152 | tf_op jit(solution)/shard_map/all_to_all | solution.py:335
  18.6 0.0 copy-start.15
  18.6 3.1 %collective-permute-start.6 = (bf16[128,2048]{1,0:T(8,128)(2,1)S(1)}, bf16[128,2048]{1,0:T(8,128)(2,1)S(1)}, u32[]{:S(2)}, u32[]{:S(2)}) collective-permute-start(bf16[128,2048]{1,0:T(8,128)(2,1)S(1)} %constant_dynamic-update-slice_fusion.refs_10_), channel_id=1, source_target_pairs={{0,48},{16,0},{32,16},{48,32},{1,49},{17,1},{33,17},{49,33},{2,50}... | collective-permute-start | bytes 1572872 | tf_op jit(solution)/shard_map/ppermute | solution.py:307
  21.7 0.0 collective-permute-start.5
  21.7 8.5 %collective-permute-done.1.refs_4_ = bf16[128,2176]{1,0:T(8,128)(2,1)S(1)} collective-permute-done((bf16[128,2176]{1,0:T(8,128)(2,1)}, bf16[128,2176]{1,0:T(8,128)(2,1)S(1)}, u32[]{:S(2)}, u32[]{:S(2)}) %collective-permute-start.1) | collective-permute-done | bytes 557088 | tf_op jit(solution)/shard_map/ppermute | solution.py:307
  30.3 3.8 %collective-permute-start.3 = (bf16[64,2176]{1,0:T(8,128)(2,1)S(1)}, bf16[64,2176]{1,0:T(8,128)(2,1)S(1)}, u32[]{:S(2)}, u32[]{:S(2)}) collective-permute-start(bf16[64,2176]{1,0:T(8,128)(2,1)S(1)} %slice.25), channel_id=1, source_target_pairs={{0,6},{2,0},{4,2},{6,4},{1,7},{3,1},{5,3},{7,5},{8,14},{10,8},{12,... | collective-permute-start | bytes 835592 | tf_op jit(solution)/shard_map/ppermute | solution.py:307
  34.1 0.0 collective-permute-done.refs_2_
  34.1 0.1 collective-permute-start.2
  34.2 0.0 collective-permute-done.6.refs_12_
  34.2 3.1 %collective-permute-start.8 = (bf16[64,2048]{1,0:T(8,128)(2,1)S(1)}, bf16[64,2048]{1,0:T(8,128)(2,1)}, u32[]{:S(2)}, u32[]{:S(2)}) collective-permute-start(bf16[64,2048]{1,0:T(8,128)(2,1)S(1)} %slice.27), channel_id=1, source_target_pairs={{0,48},{16,0},{32,16},{48,32},{1,49},{17,1},{33,17},{49,33},{2,50}... | collective-permute-start | bytes 786440 | tf_op jit(solution)/shard_map/ppermute | solution.py:307
  37.3 0.8 copy-done.14
  38.1 0.8 slice.26
  38.9 0.0 collective-permute-start.7
  38.9 3.5 %first.1 = bf16[128,2048]{1,0:T(8,128)(2,1)} custom-call(bf16[128,2048]{1,0:T(8,128)(2,1)} %pre_ref.3, f32[1,2048]{1,0:T(1,128)} %bitcast.23, bf16[128,2048]{1,0:T(8,128)(2,1)} %cot_ref.5), custom_call_target="tpu_custom_call" | custom-call | flops 1000 | bytes 1000 | tf_op jit(solution)/shard_map/first/pallas_call | solution.py:77
  42.4 0.1 collective-permute-done.3.refs_8_
  42.5 3.4 %collective-permute-done.2.refs_6_ = bf16[64,2176]{1,0:T(8,128)(2,1)S(1)} collective-permute-done((bf16[64,2176]{1,0:T(8,128)(2,1)S(1)}, bf16[64,2176]{1,0:T(8,128)(2,1)S(1)}, u32[]{:S(2)}, u32[]{:S(2)}) %collective-permute-start.2) | collective-permute-done | bytes 278560 | tf_op jit(solution)/shard_map/ppermute | solution.py:307
  45.9 2.0 %collective-permute-done.7.refs_13_ = bf16[64,2048]{1,0:T(8,128)(2,1)} collective-permute-done((bf16[64,2048]{1,0:T(8,128)(2,1)}, bf16[64,2048]{1,0:T(8,128)(2,1)}, u32[]{:S(2)}, u32[]{:S(2)}) %collective-permute-start.7) | collective-permute-done | bytes 262176 | tf_op jit(solution)/shard_map/ppermute | solution.py:307
  47.9 0.0 collective-permute-start.9
  47.9 0.5 collective-permute-start.10
  48.4 0.0 collective-permute-start.11
  48.5 0.5 collective-permute-start.12
  49.0 0.0 collective-permute-start.13
  49.0 2.9 %collective-permute-done.12.refs_7_ = bf16[64,2176]{1,0:T(8,128)(2,1)S(1)} collective-permute-done((bf16[64,2176]{1,0:T(8,128)(2,1)S(1)}, bf16[64,2176]{1,0:T(8,128)(2,1)S(1)}, u32[]{:S(2)}, u32[]{:S(2)}) %collective-permute-start.12) | collective-permute-done | bytes 278560 | tf_op jit(solution)/shard_map/ppermute | solution.py:311
  51.9 0.4 collective-permute-done.13.refs_9_
  52.3 0.0 collective-permute-done.9.refs_1_
  52.3 3.9 %weight_product.1 = (bf16[128,2176]{1,0:T(8,128)(2,1)S(1)}, bf16[128,2176]{1,0:T(8,128)(2,1)}, bf16[128,2176]{1,0:T(8,128)(2,1)}, bf16[128,2176]{1,0:T(8,128)(2,1)}) custom-call(bf16[128,2176]{1,0:T(8,128)(2,1)S(1)} %copy-done, bf16[128,2176]{1,0:T(8,128)(2,1)S(1)} %collective-permute-done.9.refs_1_, bf16[128,2176]{1,0:T(8,128)(2,1)S(1)} %collective-permute-done.refs_2_, ...), custom_call_target="tpu_custom_call" | custom-call | flops 1000 | bytes 1000 | tf_op jit(solution)/shard_map/weight_product/pallas_call | solution.py:153
  56.4 0.8 copy-done.11
  57.2 2.6 %collective-permute-start.15 = (bf16[128,2176]{1,0:T(8,128)(2,1)}, bf16[128,2176]{1,0:T(8,128)(2,1)S(1)}, u32[]{:S(2)}, u32[]{:S(2)}) collective-permute-start(bf16[128,2176]{1,0:T(8,128)(2,1)} %get-tuple-element.73), channel_id=1, source_target_pairs={{0,32},{16,48},{32,0},{48,16},{1,33},{17,49},{33,1},{49,17},{2,34}... | collective-permute-start | bytes 1671176 | tf_op jit(solution)/shard_map/ppermute | solution.py:307
  59.7 1.3 %collective-permute-start.16 = (bf16[128,2176]{1,0:T(8,128)(2,1)}, bf16[128,2176]{1,0:T(8,128)(2,1)S(1)}, u32[]{:S(2)}, u32[]{:S(2)}) collective-permute-start(bf16[128,2176]{1,0:T(8,128)(2,1)} %get-tuple-element.74), channel_id=1, source_target_pairs={{0,48},{16,0},{32,16},{48,32},{1,49},{17,1},{33,17},{49,33},{2,50}... | collective-permute-start | bytes 1671176 | tf_op jit(solution)/shard_map/ppermute | solution.py:307
  61.1 8.9 %layer_product.1 = bf16[2,8,256,128]{3,2,1,0:T(8,128)(2,1)} custom-call(bf16[128,2176]{1,0:T(8,128)(2,1)} %gate.1.refs_0_, bf16[128,2176]{1,0:T(8,128)(2,1)} %copy-done.4, bf16[128,2176]{1,0:T(8,128)(2,1)} %copy-done.3, bf16[128,2176]{1,0:T(8,128)(2,1)} %copy-done.5, bf16[128,2176]{1,0:T(8,128)(2,1)} %copy-done.2, bf16[128,2176]{1,0:T(8,128)(2,1)} %copy-done.6, ...), custom_call_target="tpu_custom_call" | custom-call | flops 1000 | bytes 1000 | tf_op jit(solution)/shard_map/layer_product/pallas_call | solution.py:206
  70.1 4.6 %all-to-all-start.1 = ((bf16[16,256,128]{2,1,0:T(8,128)(2,1)}), bf16[16,256,128]{2,1,0:T(8,128)(2,1)S(1)}, u32[]{:S(2)}, u32[]{:S(2)}) async-start(bf16[16,256,128]{2,1,0:T(8,128)(2,1)} %bitcast.19), calls=%async_computation.1 | async-start | bytes 2097152 | tf_op jit(solution)/shard_map/all_to_all | solution.py:352
  74.6 10.6 %collective-permute-done.14.two = bf16[128,2176]{1,0:T(8,128)(2,1)S(1)} collective-permute-done((bf16[128,2176]{1,0:T(8,128)(2,1)}, bf16[128,2176]{1,0:T(8,128)(2,1)S(1)}, u32[]{:S(2)}, u32[]{:S(2)}) %collective-permute-start.14) | collective-permute-done | bytes 557088 | tf_op jit(solution)/shard_map/ppermute | solution.py:307
  85.2 0.6 collective-permute-done.16.four
  85.8 0.6 fold.1
  86.4 0.0 copy-start.1
  86.4 1.2 %collective-permute-start.17 = (bf16[64,2176]{1,0:T(8,128)(2,1)S(1)}, bf16[64,2176]{1,0:T(8,128)(2,1)S(1)}, u32[]{:S(2)}, u32[]{:S(2)}) collective-permute-start(bf16[64,2176]{1,0:T(8,128)(2,1)S(1)} %get-tuple-element.76), channel_id=1, source_target_pairs={{0,8},{8,0},{1,9},{9,1},{2,10},{10,2},{3,11},{11,3},{4,12},{12,4},... | collective-permute-start | bytes 835592 | tf_op jit(solution)/shard_map/ppermute | solution.py:311
  87.6 8.9 %collective-permute-done.17.came_ref = bf16[64,2176]{1,0:T(8,128)(2,1)S(1)} collective-permute-done((bf16[64,2176]{1,0:T(8,128)(2,1)S(1)}, bf16[64,2176]{1,0:T(8,128)(2,1)S(1)}, u32[]{:S(2)}, u32[]{:S(2)}) %collective-permute-start.17) | collective-permute-done | bytes 278560 | tf_op jit(solution)/shard_map/ppermute | solution.py:311
  96.5 0.8 total.1
  97.3 0.6 slice_bitcast_fusion
  98.0 1.9 %finish.1 = bf16[128,2048]{1,0:T(8,128)(2,1)} custom-call(bf16[2,8,4,64,128]{4,3,2,1,0:T(8,128)(2,1)S(1)} %bitcast.17, bf16[128,2048]{1,0:T(8,128)(2,1)S(1)} %copy-done.1), custom_call_target="tpu_custom_call" | custom-call | flops 1000 | bytes 1000 | tf_op jit(solution)/shard_map/finish/pallas_call | solution.py:291
  (44 shorter events, 0.2 us)
Async XLA Ops:
  0.6 1.2 %copy-start.16 = (bf16[128,2048]{1,0:T(8,128)(2,1)S(1)}, bf16[128,2048]{1,0:T(8,128)(2,1)}, u32[]{:S(2)}) copy-start(bf16[128,2048]{1,0:T(8,128)(2,1)} %param.7) | copy-start | bytes 1572868
  3.2 15.3 %collective-permute-start.4 = (bf16[64,2048]{1,0:T(8,128)(2,1)S(1)}, bf16[64,2048]{1,0:T(8,128)(2,1)S(1)}, u32[]{:S(2)}, u32[]{:S(2)}) collective-permute-start(bf16[64,2048]{1,0:T(8,128)(2,1)S(1)} %convert_bitcast_fusion), channel_id=1, source_target_pairs={{0,8},{8,0},{1,9},{9,1},{2,10},{10,2},{3,11},{11,3},{4,12},{12,4},... | collective-permute-start | bytes 786440 | tf_op jit(solution)/shard_map/ppermute | solution.py:311
  10.6 19.6 %collective-permute-start.1 = (bf16[128,2176]{1,0:T(8,128)(2,1)}, bf16[128,2176]{1,0:T(8,128)(2,1)S(1)}, u32[]{:S(2)}, u32[]{:S(2)}) collective-permute-start(bf16[128,2176]{1,0:T(8,128)(2,1)} %gate.1.refs_0_), channel_id=1, source_target_pairs={{0,6},{2,0},{4,2},{6,4},{1,7},{3,1},{5,3},{7,5},{8,14},{10,8},{12,... | collective-permute-start | bytes 1671176 | tf_op jit(solution)/shard_map/ppermute | solution.py:307
  13.5 20.6 %collective-permute-start = (bf16[128,2176]{1,0:T(8,128)(2,1)}, bf16[128,2176]{1,0:T(8,128)(2,1)S(1)}, u32[]{:S(2)}, u32[]{:S(2)}) collective-permute-start(bf16[128,2176]{1,0:T(8,128)(2,1)} %gate.1.refs_0_), channel_id=1, source_target_pairs={{0,2},{2,4},{4,6},{6,0},{1,3},{3,5},{5,7},{7,1},{8,10},{10,12},{12... | collective-permute-start | bytes 1671176 | tf_op jit(solution)/shard_map/ppermute | solution.py:307
  13.5 32.4 %all-to-all-start = ((bf16[16,256,128]{2,1,0:T(8,128)(2,1)}), bf16[16,256,128]{2,1,0:T(8,128)(2,1)S(1)}, u32[]{:S(2)}, u32[]{:S(2)}) async-start(bf16[16,256,128]{2,1,0:T(8,128)(2,1)} %pad_maximum_fusion), calls=%async_computation | async-start | bytes 2097152 | tf_op jit(solution)/shard_map/all_to_all | solution.py:335
  18.6 20.2 %copy-start.15 = (bf16[128,2048]{1,0:T(8,128)(2,1)}, bf16[128,2048]{1,0:T(8,128)(2,1)S(1)}, u32[]{:S(2)}) copy-start(bf16[128,2048]{1,0:T(8,128)(2,1)S(1)} %constant_dynamic-update-slice_fusion.refs_10_) | copy-start | bytes 1572868
  18.6 15.5 %collective-permute-start.6 = (bf16[128,2048]{1,0:T(8,128)(2,1)S(1)}, bf16[128,2048]{1,0:T(8,128)(2,1)S(1)}, u32[]{:S(2)}, u32[]{:S(2)}) collective-permute-start(bf16[128,2048]{1,0:T(8,128)(2,1)S(1)} %constant_dynamic-update-slice_fusion.refs_10_), channel_id=1, source_target_pairs={{0,48},{16,0},{32,16},{48,32},{1,49},{17,1},{33,17},{49,33},{2,50}... | collective-permute-start | bytes 1572872 | tf_op jit(solution)/shard_map/ppermute | solution.py:307
  21.7 15.6 %collective-permute-start.5 = (bf16[128,2048]{1,0:T(8,128)(2,1)S(1)}, bf16[128,2048]{1,0:T(8,128)(2,1)S(1)}, u32[]{:S(2)}, u32[]{:S(2)}) collective-permute-start(bf16[128,2048]{1,0:T(8,128)(2,1)S(1)} %constant_dynamic-update-slice_fusion.refs_10_), channel_id=1, source_target_pairs={{0,16},{16,32},{32,48},{48,0},{1,17},{17,33},{33,49},{49,1},{2,18}... | collective-permute-start | bytes 1572872 | tf_op jit(solution)/shard_map/ppermute | solution.py:307
  30.2 22.1 %copy-start.2 = (bf16[128,2176]{1,0:T(8,128)(2,1)}, bf16[128,2176]{1,0:T(8,128)(2,1)S(1)}, u32[]{:S(2)}) copy-start(bf16[128,2176]{1,0:T(8,128)(2,1)S(1)} %collective-permute-done.1.refs_4_) | copy-start | bytes 1671172
  30.3 12.2 %collective-permute-start.3 = (bf16[64,2176]{1,0:T(8,128)(2,1)S(1)}, bf16[64,2176]{1,0:T(8,128)(2,1)S(1)}, u32[]{:S(2)}, u32[]{:S(2)}) collective-permute-start(bf16[64,2176]{1,0:T(8,128)(2,1)S(1)} %slice.25), channel_id=1, source_target_pairs={{0,6},{2,0},{4,2},{6,4},{1,7},{3,1},{5,3},{7,5},{8,14},{10,8},{12,... | collective-permute-start | bytes 835592 | tf_op jit(solution)/shard_map/ppermute | solution.py:307
  34.1 18.3 %copy-start.3 = (bf16[128,2176]{1,0:T(8,128)(2,1)}, bf16[128,2176]{1,0:T(8,128)(2,1)S(1)}, u32[]{:S(2)}) copy-start(bf16[128,2176]{1,0:T(8,128)(2,1)S(1)} %collective-permute-done.refs_2_) | copy-start | bytes 1671172
  34.1 11.8 %collective-permute-start.2 = (bf16[64,2176]{1,0:T(8,128)(2,1)S(1)}, bf16[64,2176]{1,0:T(8,128)(2,1)S(1)}, u32[]{:S(2)}, u32[]{:S(2)}) collective-permute-start(bf16[64,2176]{1,0:T(8,128)(2,1)S(1)} %slice.24), channel_id=1, source_target_pairs={{0,2},{2,4},{4,6},{6,0},{1,3},{3,5},{5,7},{7,1},{8,10},{10,12},{12... | collective-permute-start | bytes 835592 | tf_op jit(solution)/shard_map/ppermute | solution.py:307
  34.2 4.7 %copy-start.13 = (bf16[128,2048]{1,0:T(8,128)(2,1)}, bf16[128,2048]{1,0:T(8,128)(2,1)S(1)}, u32[]{:S(2)}) copy-start(bf16[128,2048]{1,0:T(8,128)(2,1)S(1)} %collective-permute-done.6.refs_12_) | copy-start | bytes 1572868
  34.2 11.7 %collective-permute-start.8 = (bf16[64,2048]{1,0:T(8,128)(2,1)S(1)}, bf16[64,2048]{1,0:T(8,128)(2,1)}, u32[]{:S(2)}, u32[]{:S(2)}) collective-permute-start(bf16[64,2048]{1,0:T(8,128)(2,1)S(1)} %slice.27), channel_id=1, source_target_pairs={{0,48},{16,0},{32,16},{48,32},{1,49},{17,1},{33,17},{49,33},{2,50}... | collective-permute-start | bytes 786440 | tf_op jit(solution)/shard_map/ppermute | solution.py:307
  37.3 0.8 copy-start.14
  38.9 9.1 %copy-start = (bf16[128,2176]{1,0:T(8,128)(2,1)S(1)}, bf16[128,2176]{1,0:T(8,128)(2,1)}, u32[]{:S(2)}) copy-start(bf16[128,2176]{1,0:T(8,128)(2,1)} %gate.1.refs_0_) | copy-start | bytes 1671172
  38.9 9.1 %collective-permute-start.7 = (bf16[64,2048]{1,0:T(8,128)(2,1)}, bf16[64,2048]{1,0:T(8,128)(2,1)}, u32[]{:S(2)}, u32[]{:S(2)}) collective-permute-start(bf16[64,2048]{1,0:T(8,128)(2,1)} %slice.26), channel_id=1, source_target_pairs={{0,16},{16,32},{32,48},{48,0},{1,17},{17,33},{33,49},{49,1},{2,18}... | collective-permute-start | bytes 786440 | tf_op jit(solution)/shard_map/ppermute | solution.py:307
  42.5 13.8 %copy-start.7 = (bf16[64,2176]{1,0:T(8,128)(2,1)}, bf16[64,2176]{1,0:T(8,128)(2,1)S(1)}, u32[]{:S(2)}) copy-start(bf16[64,2176]{1,0:T(8,128)(2,1)S(1)} %collective-permute-done.3.refs_8_) | copy-start | bytes 835588
  45.9 10.4 %copy-start.8 = (bf16[64,2176]{1,0:T(8,128)(2,1)}, bf16[64,2176]{1,0:T(8,128)(2,1)S(1)}, u32[]{:S(2)}) copy-start(bf16[64,2176]{1,0:T(8,128)(2,1)S(1)} %collective-permute-done.2.refs_6_) | copy-start | bytes 835588
  47.9 4.4 %collective-permute-start.9 = (bf16[128,2176]{1,0:T(8,128)(2,1)S(1)}, bf16[128,2176]{1,0:T(8,128)(2,1)S(1)}, u32[]{:S(2)}, u32[]{:S(2)}) collective-permute-start(bf16[128,2176]{1,0:T(8,128)(2,1)S(1)} %copy-done), channel_id=1, source_target_pairs={{0,1},{1,0},{2,3},{3,2},{4,5},{5,4},{6,7},{7,6},{8,9},{9,8},{10,11... | collective-permute-start | bytes 1671176 | tf_op jit(solution)/shard_map/ppermute | solution.py:311
  47.9 4.4 %collective-permute-start.10 = (bf16[128,2176]{1,0:T(8,128)(2,1)S(1)}, bf16[128,2176]{1,0:T(8,128)(2,1)S(1)}, u32[]{:S(2)}, u32[]{:S(2)}) collective-permute-start(bf16[128,2176]{1,0:T(8,128)(2,1)S(1)} %collective-permute-done.refs_2_), channel_id=1, source_target_pairs={{0,1},{1,0},{2,3},{3,2},{4,5},{5,4},{6,7},{7,6},{8,9},{9,8},{10,11... | collective-permute-start | bytes 1671176 | tf_op jit(solution)/shard_map/ppermute | solution.py:311
  48.4 3.9 %collective-permute-start.11 = (bf16[128,2176]{1,0:T(8,128)(2,1)S(1)}, bf16[128,2176]{1,0:T(8,128)(2,1)S(1)}, u32[]{:S(2)}, u32[]{:S(2)}) collective-permute-start(bf16[128,2176]{1,0:T(8,128)(2,1)S(1)} %collective-permute-done.1.refs_4_), channel_id=1, source_target_pairs={{0,1},{1,0},{2,3},{3,2},{4,5},{5,4},{6,7},{7,6},{8,9},{9,8},{10,11... | collective-permute-start | bytes 1671176 | tf_op jit(solution)/shard_map/ppermute | solution.py:311
  48.5 3.4 %collective-permute-start.12 = (bf16[64,2176]{1,0:T(8,128)(2,1)S(1)}, bf16[64,2176]{1,0:T(8,128)(2,1)S(1)}, u32[]{:S(2)}, u32[]{:S(2)}) collective-permute-start(bf16[64,2176]{1,0:T(8,128)(2,1)S(1)} %collective-permute-done.2.refs_6_), channel_id=1, source_target_pairs={{0,1},{1,0},{2,3},{3,2},{4,5},{5,4},{6,7},{7,6},{8,9},{9,8},{10,11... | collective-permute-start | bytes 835592 | tf_op jit(solution)/shard_map/ppermute | solution.py:311
  49.0 3.3 %collective-permute-start.13 = (bf16[64,2176]{1,0:T(8,128)(2,1)S(1)}, bf16[64,2176]{1,0:T(8,128)(2,1)S(1)}, u32[]{:S(2)}, u32[]{:S(2)}) collective-permute-start(bf16[64,2176]{1,0:T(8,128)(2,1)S(1)} %collective-permute-done.3.refs_8_), channel_id=1, source_target_pairs={{0,1},{1,0},{2,3},{3,2},{4,5},{5,4},{6,7},{7,6},{8,9},{9,8},{10,11... | collective-permute-start | bytes 835592 | tf_op jit(solution)/shard_map/ppermute | solution.py:311
  51.9 4.4 %copy-start.9 = (bf16[64,2176]{1,0:T(8,128)(2,1)}, bf16[64,2176]{1,0:T(8,128)(2,1)S(1)}, u32[]{:S(2)}) copy-start(bf16[64,2176]{1,0:T(8,128)(2,1)S(1)} %collective-permute-done.12.refs_7_) | copy-start | bytes 835588
  52.3 4.0 %copy-start.10 = (bf16[64,2176]{1,0:T(8,128)(2,1)}, bf16[64,2176]{1,0:T(8,128)(2,1)S(1)}, u32[]{:S(2)}) copy-start(bf16[64,2176]{1,0:T(8,128)(2,1)S(1)} %collective-permute-done.13.refs_9_) | copy-start | bytes 835588
  52.3 4.0 %copy-start.4 = (bf16[128,2176]{1,0:T(8,128)(2,1)}, bf16[128,2176]{1,0:T(8,128)(2,1)S(1)}, u32[]{:S(2)}) copy-start(bf16[128,2176]{1,0:T(8,128)(2,1)S(1)} %collective-permute-done.9.refs_1_) | copy-start | bytes 1671172
  52.3 4.0 %copy-start.5 = (bf16[128,2176]{1,0:T(8,128)(2,1)}, bf16[128,2176]{1,0:T(8,128)(2,1)S(1)}, u32[]{:S(2)}) copy-start(bf16[128,2176]{1,0:T(8,128)(2,1)S(1)} %collective-permute-done.10.refs_3_) | copy-start | bytes 1671172
  52.3 4.0 %copy-start.6 = (bf16[128,2176]{1,0:T(8,128)(2,1)}, bf16[128,2176]{1,0:T(8,128)(2,1)S(1)}, u32[]{:S(2)}) copy-start(bf16[128,2176]{1,0:T(8,128)(2,1)S(1)} %collective-permute-done.11.refs_5_) | copy-start | bytes 1671172
  56.4 0.8 copy-start.11
  57.2 28.0 %collective-permute-start.14 = (bf16[128,2176]{1,0:T(8,128)(2,1)}, bf16[128,2176]{1,0:T(8,128)(2,1)S(1)}, u32[]{:S(2)}, u32[]{:S(2)}) collective-permute-start(bf16[128,2176]{1,0:T(8,128)(2,1)} %get-tuple-element.72), channel_id=1, source_target_pairs={{0,16},{16,32},{32,48},{48,0},{1,17},{17,33},{33,49},{49,1},{2,18}... | collective-permute-start | bytes 1671176 | tf_op jit(solution)/shard_map/ppermute | solution.py:307
  57.2 28.0 %collective-permute-start.15 = (bf16[128,2176]{1,0:T(8,128)(2,1)}, bf16[128,2176]{1,0:T(8,128)(2,1)S(1)}, u32[]{:S(2)}, u32[]{:S(2)}) collective-permute-start(bf16[128,2176]{1,0:T(8,128)(2,1)} %get-tuple-element.73), channel_id=1, source_target_pairs={{0,32},{16,48},{32,0},{48,16},{1,33},{17,49},{33,1},{49,17},{2,34}... | collective-permute-start | bytes 1671176 | tf_op jit(solution)/shard_map/ppermute | solution.py:307
  59.7 26.1 %collective-permute-start.16 = (bf16[128,2176]{1,0:T(8,128)(2,1)}, bf16[128,2176]{1,0:T(8,128)(2,1)S(1)}, u32[]{:S(2)}, u32[]{:S(2)}) collective-permute-start(bf16[128,2176]{1,0:T(8,128)(2,1)} %get-tuple-element.74), channel_id=1, source_target_pairs={{0,48},{16,0},{32,16},{48,32},{1,49},{17,1},{33,17},{49,33},{2,50}... | collective-permute-start | bytes 1671176 | tf_op jit(solution)/shard_map/ppermute | solution.py:307
  70.0 15.8 %copy-start.12 = (bf16[128,2176]{1,0:T(8,128)(2,1)S(1)}, bf16[128,2176]{1,0:T(8,128)(2,1)}, u32[]{:S(2)}) copy-start(bf16[128,2176]{1,0:T(8,128)(2,1)} %copy-done.11) | copy-start | bytes 1671172
  70.1 27.9 %all-to-all-start.1 = ((bf16[16,256,128]{2,1,0:T(8,128)(2,1)}), bf16[16,256,128]{2,1,0:T(8,128)(2,1)S(1)}, u32[]{:S(2)}, u32[]{:S(2)}) async-start(bf16[16,256,128]{2,1,0:T(8,128)(2,1)} %bitcast.19), calls=%async_computation.1 | async-start | bytes 2097152 | tf_op jit(solution)/shard_map/all_to_all | solution.py:352
  86.4 11.6 %copy-start.1 = (bf16[128,2048]{1,0:T(8,128)(2,1)S(1)}, bf16[128,2048]{1,0:T(8,128)(2,1)}, u32[]{:S(2)}) copy-start(bf16[128,2048]{1,0:T(8,128)(2,1)} %cot_ref.5) | copy-start | bytes 1572868
  86.4 10.1 %collective-permute-start.17 = (bf16[64,2176]{1,0:T(8,128)(2,1)S(1)}, bf16[64,2176]{1,0:T(8,128)(2,1)S(1)}, u32[]{:S(2)}, u32[]{:S(2)}) collective-permute-start(bf16[64,2176]{1,0:T(8,128)(2,1)S(1)} %get-tuple-element.76), channel_id=1, source_target_pairs={{0,8},{8,0},{1,9},{9,1},{2,10},{10,2},{3,11},{11,3},{4,12},{12,4},... | collective-permute-start | bytes 835592 | tf_op jit(solution)/shard_map/ppermute | solution.py:311
